TPU v7x, 32 devices: a whole 2x2x4 slice. The times are simulated.
32 devices in a mesh: ctx: 8 (over z, y), head: 4 (over x, core).
Axes of the slice: x: 2, y: 2, z: 4, core: 2. Of those that a mesh axis runs over, the one named last changes fastest.
Arguments:
- activations: bfloat16 [4096, 2048], P(('ctx', 'head')), may hold values from -6 to 6
- w_in: bfloat16 [2048, 14336], P('ctx', 'head'), may hold values from -0.125 to 0.125
- w_beta: bfloat16 [2048, 48], P('ctx', 'head'), may hold values from -0.0625 to 0.0625
- beta_bias: float32 [48], P('head'), may hold values from -2 to 10
- head_gain: float32 [2048], P('head'), may hold values from 0.1 to 1.9
- w_out: bfloat16 [2048, 2048], P('head'), may hold values from -0.125 to 0.125
Outputs:
- mixed_out: bfloat16 [4096, 2048], P(('ctx', 'head'))
All inputs are finite; a program needn't handle non-finite values.
Results may differ from a plain program's by a relative error of at most 0.015.
The roundings to bfloat16 on the way count: a program that leaves them out, or rounds other values in their place, can miss the bound.
Values may be sent and summed in bfloat16 or wider, within the bound.
A program may use at most 128 MiB of HBM per device.

v0:
```python
import jax
import jax.numpy as jnp
from jax import lax
from jax.sharding import PartitionSpec as P

DK = 128
NF = 3
BLOCK = 64


EPSILON = 1e-06
PRECISE = lax.Precision.HIGHEST


def passed_along(block, axis, distance):
    devices = range(lax.axis_size(axis))
    route = [(i - distance, i) for i in devices if i - distance in devices]
    return lax.ppermute(block, axis, route)


def matmul(form, left, right):
    return jnp.einsum(form, left, right, precision=PRECISE)


def block_terms(unit_keys, values, beta_rows):
    gram_mat = matmul("...id,...jd->...ij", unit_keys, unit_keys)
    length = unit_keys.shape[-2]
    strict = jnp.tril(jnp.ones((length, length), jnp.float32), -1)
    system = jnp.eye(length, dtype=jnp.float32) + strict * beta_rows[..., :, None] * gram_mat
    right_side = jnp.concatenate(
        [beta_rows[..., None] * unit_keys, beta_rows[..., None] * values], axis=-1
    )
    solved = jax.scipy.linalg.solve_triangular(system, right_side, lower=True, unit_diagonal=True)
    split_at = unit_keys.shape[-1]
    return (solved[..., :split_at], solved[..., split_at:])


def compose(earlier, later):
    return (
        matmul("hij,hjk->hik", earlier[0], later[0]),
        matmul("hij,hjk->hik", earlier[1], later[0]) + later[1],
    )


def block_outputs(queries, scores, w_rows, u_rows, starts):
    fresh_rows = u_rows - matmul("hnjd,hned->hnje", w_rows, starts)
    return matmul("hnid,hned->hnie", queries, starts) + matmul(
        "hnij,hnje->hnie", scores, fresh_rows
    )


def shards(activations, w_in, w_beta, beta_bias, head_gain, w_out):
    gathered = lax.all_gather(activations, "head", axis=0, tiled=True)
    seg_len = gathered.shape[0]
    heads_here = head_gain.shape[0] // DK
    pieces = (
        lax.all_gather(w_in, "ctx", axis=0, tiled=True),
        lax.all_gather(w_beta, "ctx", axis=0, tiled=True),
    )
    proj_sum = jnp.dot(gathered, pieces[0], preferred_element_type=jnp.float32)
    logit_sum = jnp.dot(gathered, pieces[1], preferred_element_type=jnp.float32)
    projected = lax.optimization_barrier(proj_sum.astype(jnp.bfloat16)).astype(jnp.float32)
    beta_rows = 2.0 / (1.0 + jnp.exp(-(logit_sum + beta_bias)))
    nblocks = seg_len // BLOCK
    factor_len = BLOCK * NF
    pieces = projected.reshape(seg_len, heads_here, 1 + 2 * NF, DK)
    queries = jnp.transpose(pieces[:, :, 0], (1, 0, 2)).reshape(heads_here, nblocks, BLOCK, DK)
    raw_keys = pieces[:, :, 1 : 1 + NF]
    unit_keys = raw_keys / jnp.sqrt(jnp.sum(raw_keys * raw_keys, axis=-1, keepdims=True) + EPSILON)
    unit_keys = jnp.transpose(unit_keys, (1, 0, 2, 3)).reshape(heads_here, nblocks, factor_len, DK)
    values = jnp.transpose(pieces[:, :, 1 + NF :], (1, 0, 2, 3)).reshape(
        heads_here, nblocks, factor_len, DK
    )
    beta_rows = jnp.transpose(beta_rows.reshape(seg_len, heads_here, NF), (1, 0, 2)).reshape(
        heads_here, nblocks, factor_len
    )
    w_rows, u_rows = block_terms(unit_keys, values, beta_rows)
    causal = (jnp.arange(factor_len)[None, :] <= NF * jnp.arange(BLOCK)[:, None] + NF - 1).astype(
        jnp.float32
    )
    scores = matmul("hnid,hnjd->hnij", queries, unit_keys) * causal
    unit_mats = jnp.broadcast_to(jnp.eye(DK, dtype=jnp.float32), (heads_here, DK, DK))
    zero_mats = jnp.zeros((heads_here, DK, DK), jnp.float32)
    transits = unit_mats[:, None] - matmul("hnjd,hnje->hnde", w_rows, unit_keys)
    injects = matmul("hnje,hnjd->hned", u_rows, unit_keys)
    transit_seq = jnp.moveaxis(transits, 1, 0)
    inject_seq = jnp.moveaxis(injects, 1, 0)

    def fold_prefix(carried, blockwise):
        return (compose(carried, blockwise), carried)

    totals, prefixes = lax.scan(fold_prefix, (unit_mats, zero_mats), (transit_seq, inject_seq))

    def relay(turn_index, incoming):
        leaving = matmul("hed,hdf->hef", incoming, totals[0]) + totals[1]
        return passed_along(leaving.astype(jnp.bfloat16), "ctx", 1).astype(leaving.dtype)

    entering = lax.fori_loop(0, lax.axis_size("ctx") - 1, relay, jnp.zeros_like(totals[1]))

    def advance(carried, blockwise):
        return (matmul("hed,hdf->hef", carried, blockwise[0]) + blockwise[1], carried)

    ignored, starts = lax.scan(advance, entering, (transit_seq, inject_seq))
    attended = block_outputs(queries, scores, w_rows, u_rows, jnp.moveaxis(starts, 0, 1))
    attended = attended.reshape(heads_here, seg_len, DK)
    scale = 1.0 / jnp.sqrt(jnp.mean(attended * attended, axis=-1, keepdims=True) + EPSILON)
    normed = (attended * scale * head_gain.reshape(heads_here, 1, DK)).astype(jnp.bfloat16)
    normed = jnp.transpose(normed, (1, 0, 2)).reshape(seg_len, heads_here * DK)
    return lax.psum_scatter(
        jnp.dot(normed, w_out, preferred_element_type=jnp.float32).astype(jnp.bfloat16),
        "head",
        scatter_dimension=0,
        tiled=True,
    )


def solution(mesh):
    return jax.shard_map(
        shards,
        mesh=mesh,
        in_specs=(
            P(("ctx", "head"), None),
            P("ctx", "head"),
            P("ctx", "head"),
            P("head"),
            P("head"),
            P("head", None),
        ),
        out_specs=P(("ctx", "head"), None),
        check_vma=False,
    )
```

profile of v0, /device:TPU:21, one launch (start us, length us, event | category | flops | bytes accessed | tf_op | source)
XLA Modules:
  0.0 1124.2 jit_solution(9912607747555828433)
XLA Ops:
  8.2 23.1 %all_gather.11 = bf16[2048,12]{0,1:T(8,128)(2,1)S(1)} all-gather(bf16[256,12]{0,1:T(8,128)(2,1)} %param.14), channel_id=1, replica_groups=mesh['ctx'=8,'head'=4] {'ctx'}, dimensions={0}, use_global_device_ids=true | all-gather | bytes 55296 | tf_op jit(solution)/shard_map/all_gather | solution.py:58
  33.5 2.3 fusion.56
  35.8 1.4 copy.32
  37.2 1.7 mul.74
  38.9 195.7 %all-gather.5.cloned.1.call-done = bf16[2048,3584]{1,0:T(8,128)(2,1)} async-done(((bf16[256,3584]{1,0:T(8,128)(2,1)}), bf16[2048,3584]{1,0:T(8,128)(2,1)}) %all-gather.5.cloned.1.call-update) | async-done | bytes 14680080 | tf_op jit(solution)/shard_map/all_gather | solution.py:57
  234.6 12.9 %convolution_convert_fusion = bf16[512,3584]{1,0:T(8,128)(2,1)} fusion(bf16[512,2048]{1,0:T(8,128)(2,1)} %all-gather.3.cloned.1.call-done, bf16[2048,3584]{1,0:T(8,128)(2,1)} %all-gather.5.cloned.1.call-done), kind=kOutput, calls=%fused_computation.30 | convolution fusion | flops 7518027776 | bytes 20447232 | tf_op jit(solution)/shard_map/dot_general | solution.py:60
  247.5 5.9 copy.29
  254.5 3.1 reshape.117
  258.0 3.4 slice_bitcast_fusion
  261.4 4.9 copy.33
  266.3 10.4 select_add_fusion
  278.0 1.8 copy-done.13
  279.7 1.5 slice_bitcast_fusion.3
  281.2 4.9 copy.38
  286.1 5.6 copy_multiply_fusion
  293.5 2.3 pad_maximum_fusion
  295.9 630.7 %custom-call.4 = f32[4,8,2,128,128]{3,4,2,1,0:T(8,128)} custom-call(f32[4,8,2,128,128]{4,3,2,1,0:T(8,128)} %pad_maximum_fusion), custom_call_target="InvertDiagBlocksLowerTriangular" | custom-call | tf_op jit(solution)/shard_map/jit(_solve_triangular)/vmap(vmap())/triangular_solve | solution.py:33
  926.5 7.1 fusion.21
  933.7 4.8 fusion.57
  938.5 3.5 fusion.34
  942.0 8.5 subtract_bitcast_fusion
  950.5 8.2 fusion.45
  959.7 2.9 copy.44
  962.7 2.9 copy.45
  965.6 23.1 %while.39 = (s32[]{:T(128)}, f32[4,128,128]{1,2,0:T(8,128)S(1)}, f32[4,128,128]{1,2,0:T(8,128)S(1)}, f32[8,4,128,128]{2,3,1,0:T(8,128)}, f32[8,4,128,128]{2,3,1,0:T(8,128)}, /*index=5*/s32[]{:T(128)}, s32[]{:T(128)}) while((s32[]{:T(128)}, f32[4,128,128]{1,2,0:T(8,128)S(1)}, f32[4,128,128]{1,2,0:T(8,128)S(1)}, ...), condition=%wide.region_2.3_spmd.clone, body=%wide.region_1.2_spmd.clone.sunk | while | flops 201457664 | bytes 2885218 | solution.py:92
  967.0 1.4 fusion.104
  968.5 1.3 convolution_bitcast_fusion.4
  969.9 1.4 fusion.104
  972.7 1.4 fusion.104
  975.6 1.4 fusion.104
  978.4 1.4 fusion.104
  981.3 1.4 fusion.104
  984.2 1.4 fusion.104
  987.0 1.4 fusion.104
  988.9 50.3 %while.40 = (s32[]{:T(128)}, f32[4,128,128]{2,1,0:T(8,128)S(1)}, f32[4,128,128]{2,1,0:T(8,128)S(1)}, f32[4,128,128]{2,1,0:T(8,128)S(1)}, s32[]{:T(128)}, /*index=5*/s32[]{:T(128)}) while((s32[]{:T(128)}, f32[4,128,128]{2,1,0:T(8,128)S(1)}, f32[4,128,128]{2,1,0:T(8,128)S(1)}, f32[4,128,128]{2,1,0:T(8,128)S(1)}, s32[]{:T(128)}, ...), condition=%wide.region_4.5_spmd.clone, body=%wide.region_3.4_spmd.clone.sunk | while | flops 100925440 | bytes 1835127 | solution.py:98
  989.4 3.6 collective-permute-start
  993.0 2.4 collective-permute-done
  995.8 5.0 collective-permute-start
  1000.8 1.9 collective-permute-done
  1003.2 4.7 collective-permute-start
  1007.9 1.9 collective-permute-done
  1010.3 4.7 collective-permute-start
  1015.0 1.9 collective-permute-done
  1017.3 4.7 collective-permute-start
  1022.0 1.9 collective-permute-done
  1024.4 4.7 collective-permute-start
  1029.1 1.9 collective-permute-done
  1031.4 4.7 collective-permute-start
  1036.1 3.1 collective-permute-done
  1039.4 17.7 %while.38 = (s32[]{:T(128)}, f32[4,128,128]{1,2,0:T(8,128)S(1)}, f32[8,4,128,128]{2,3,1,0:T(8,128)}, f32[8,4,128,128]{2,3,1,0:T(8,128)}, f32[8,4,128,128]{2,3,1,0:T(8,128)}, /*index=5*/s32[]{:T(128)}) while((s32[]{:T(128)}, f32[4,128,128]{1,2,0:T(8,128)S(1)}, f32[8,4,128,128]{2,3,1,0:T(8,128)}, f32[8,4,128,128]{2,3,1,0:T(8,128)}, ...), condition=%wide.region_6.7_spmd, body=%wide.region_5.6_spmd.sunk | while | flops 100728832 | bytes 2098257 | solution.py:103
  1040.2 1.4 fusion.99
  1042.4 1.4 fusion.99
  1044.6 1.4 fusion.99
  1046.8 1.4 fusion.99
  1049.0 1.4 fusion.99
  1051.3 1.4 fusion.99
  1053.5 1.4 fusion.99
  1055.7 1.4 fusion.99
  1057.1 5.0 fusion.39
  1064.1 3.1 fusion.30
  1067.3 4.8 multiply_reduce_fusion.1
  1072.1 1.6 copy.52
  1073.9 2.6 convolution_convert_fusion.1
  1076.5 40.8 %reduce-scatter.2.cloned.1.call-done = bf16[128,2048]{1,0:T(8,128)(2,1)} async-done(((bf16[512,2048]{1,0:T(8,128)(2,1)}), bf16[128,2048]{1,0:T(8,128)(2,1)}) %reduce-scatter.2.cloned.1.call-update) | async-done | bytes 524304 | tf_op jit(solution)/shard_map/reduce_scatter | solution.py:109
  (120 shorter events, 30.7 us)
Async XLA Ops:
  6.5 1067.3 %copy-start = (bf16[512,2048]{1,0:T(8,128)(2,1)S(1)}, bf16[512,2048]{1,0:T(8,128)(2,1)}, u32[]{:S(2)}) copy-start(bf16[512,2048]{1,0:T(8,128)(2,1)} %param.17) | copy-start | bytes 6291460
  6.5 27.0 %copy-start.15 = (f32[12]{0:T(128)S(1)}, f32[12]{0:T(128)}, u32[]{:S(2)}) copy-start(f32[12]{0:T(128)} %param.15) | copy-start | bytes 148
  6.5 27.0 %all-gather.3.cloned.1.call-start = ((), (), s32[]{:S(2)}) async-start(), calls=%async_computation.1 | async-start | bytes 2621440 | tf_op jit(solution)/shard_map/all_gather | solution.py:53
  7.3 227.4 %all-gather.5.cloned.1.call-start = ((), (), s32[]{:S(2)}) async-start(), calls=%async_computation.2 | async-start | bytes 16515072 | tf_op jit(solution)/shard_map/all_gather | solution.py:57
  8.0 1109.3 %reduce-scatter.2.cloned.1.call-start = ((), (), s32[]{:S(2)}) async-start(), calls=%async_computation.3 | async-start | bytes 2621440 | tf_op jit(solution)/shard_map/reduce_scatter | solution.py:109
  276.7 3.0 copy-start.13
  286.1 5.8 copy-start.12
  291.9 1.6 copy-start.10
  933.7 16.8 %copy-start.1 = (f32[4,8,128,256]{3,2,1,0:T(8,128)}, f32[4,8,128,256]{3,2,1,0:T(8,128)S(1)}, u32[]{:S(2)}) copy-start(f32[4,8,128,256]{3,2,1,0:T(8,128)S(1)} %fusion.21) | copy-start | bytes 12582916
  933.7 4.8 copy-start.7
  933.7 4.8 copy-start.8
  938.5 3.5 copy-start.3
  942.0 8.5 copy-start.5
  989.4 6.0 collective-permute-start
  995.8 6.9 collective-permute-start
  1003.2 6.6 collective-permute-start
  1010.3 6.6 collective-permute-start
  1017.3 6.6 collective-permute-start
  1024.4 6.6 collective-permute-start
  1031.4 7.8 collective-permute-start
  1057.1 5.1 copy-start.9
  1057.1 5.1 copy-start.11
  1062.2 1.9 copy-start.4
  1062.2 5.0 copy-start.6
  1064.1 3.2 copy-start.2
  1067.2 6.5 copy-start.14
Sparse Core Ops, SparseCore 0:
  8.9 23.9 all-gather.2
  35.2 199.4 all-gather.4
  1076.6 40.5 reduce-scatter.1
where the time goes:
time: 1140 us; the launch traced here: 1120 us
  other arithmetic  649 us (57%)
  waiting for transfers between devices  253 us (22%)
  matrix products  111 us (10%)
  local copies, waits for them, and re-layouts  41.6 us (4%)
  starting transfers between devices  32.1 us (3%)
  blocking collectives  23.1 us (2%)
  between operations  13.9 us (1%)
    another operation x8, other arithmetic, block_terms(): jax.scipy.linalg.solve_triangular(system, right_side, lower=True, unit_di...  635 us
    all_gather x1, waiting for transfers between devices, shards(): lax.all_gather(w_in, 'ctx', axis=0, tiled=True)  196 us
    dot_general x38, matrix products, matmul(): return jnp.einsum(form, left, right, precision=PRECISE)  77.6 us
    reduce_scatter x1, waiting for transfers between devices, shards(): lax.psum_scatter(jnp.dot(normed, w_out, preferred_element_type=jnp.float3...  40.8 us
    ppermute x7, starting transfers between devices, passed_along(): return lax.ppermute(block, axis, route)  32 us
    all_gather x1, blocking collectives, shards(): lax.all_gather(w_beta, 'ctx', axis=0, tiled=True)  23.1 us
  transfers between devices with their start and end apart: 10, of which 9 were waited for; matrix products, arithmetic and copies ran while one was open for 1% of the time, Pallas kernels for 0%

commit v1 on v0

v1 whole, which is shorter than its diff:
```python
import functools

import jax
import jax.numpy as jnp
from jax import lax
from jax.experimental import pallas as pl
from jax.experimental.pallas import tpu as pltpu
from jax.sharding import PartitionSpec as P

DK = 128
NF = 3
BLOCK = 64
HEADS_DEV = 4
FACTORS = BLOCK * NF
COLS = (1 + 2 * NF) * DK
EPSILON = 1e-06
PRECISE = lax.Precision.HIGHEST
MESH = pl.DeviceIdType.MESH
BF16 = jnp.bfloat16
F32 = jnp.float32


def gather_kernel(ctx_n, head_n, heads, w_in, w_beta, acts, w_out, w_all, beta_all, acts_all, out_all,
                  local_sem, w_send, w_recv, b_send, b_recv, a_send, a_recv, o_send, o_recv):
    ctx, head = lax.axis_index("ctx"), lax.axis_index("head")
    place = lax.rem(ctx, heads)
    base = ctx - place
    team = [(dc, dg) for dc in range(heads) for dg in range(head_n) if (dc, dg) != (0, 0)]

    def teammate(dc, dg):
        return (base + lax.rem(place + dc, heads), lax.rem(head + dg, head_n))

    barrier = pltpu.get_barrier_semaphore()
    for off in range(1, ctx_n):
        pl.semaphore_signal(barrier, inc=1, device_id=(lax.rem(ctx + off, ctx_n), head), device_id_type=MESH)
    for dc, dg in team:
        pl.semaphore_signal(barrier, inc=1, device_id=teammate(dc, dg), device_id_type=MESH)
    pl.semaphore_wait(barrier, ctx_n - 1 + len(team))

    def columns(of):
        return w_in.at[:, pl.ds(pl.multiple_of(lax.rem(of, heads) * COLS, DK), COLS)]

    copies = []

    def send(src, dst, ssem, rsem, device):
        copy = pltpu.make_async_remote_copy(src_ref=src, dst_ref=dst, send_sem=ssem, recv_sem=rsem,
                                            device_id=device, device_id_type=MESH)
        copy.start()
        copies.append(copy)

    order = sorted(range(1, ctx_n), key=lambda off: -min(off, ctx_n - off))
    for off in order:
        to = lax.rem(ctx + off, ctx_n)
        send(columns(to), w_all.at[ctx], w_send.at[off], w_recv.at[off], (to, head))
        send(w_beta, beta_all.at[ctx], b_send.at[off], b_recv.at[off], (to, head))
    for n, (dc, dg) in enumerate(team):
        send(acts, acts_all.at[place * head_n + head], a_send.at[n], a_recv.at[n], teammate(dc, dg))
    for off in range(1, head_n):
        send(w_out, out_all.at[head], o_send.at[off], o_recv.at[off], (ctx, lax.rem(head + off, head_n)))
    own = [
        pltpu.make_async_copy(columns(ctx), w_all.at[ctx], local_sem.at[0]),
        pltpu.make_async_copy(w_beta, beta_all.at[ctx], local_sem.at[1]),
        pltpu.make_async_copy(acts, acts_all.at[place * head_n + head], local_sem.at[2]),
        pltpu.make_async_copy(w_out, out_all.at[head], local_sem.at[3]),
    ]
    for copy in own:
        copy.start()
    for copy in own + copies:
        copy.wait()


def gather_all(ctx_n, head_n, heads, w_in, w_beta, acts, w_out):
    team = heads * head_n
    sems = [pltpu.SemaphoreType.DMA((n,)) for n in (4, ctx_n, ctx_n, ctx_n, ctx_n, team, team, head_n, head_n)]
    return pl.pallas_call(
        functools.partial(gather_kernel, ctx_n, head_n, heads),
        out_shape=(
            jax.ShapeDtypeStruct((ctx_n, w_in.shape[0], COLS), BF16),
            jax.ShapeDtypeStruct((ctx_n,) + w_beta.shape, BF16),
            jax.ShapeDtypeStruct((team,) + acts.shape, BF16),
            jax.ShapeDtypeStruct((head_n,) + w_out.shape, BF16),
        ),
        in_specs=[pl.BlockSpec(memory_space=pl.ANY)] * 4,
        out_specs=(pl.BlockSpec(memory_space=pl.ANY),) * 4,
        scratch_shapes=sems,
        compiler_params=pltpu.CompilerParams(collective_id=0, has_side_effects=True),
    )(w_in, w_beta, acts, w_out)


def exchange_kernel(head_n, heads, rows, mine, got, local_sem, send_sem, recv_sem):
    ctx, head = lax.axis_index("ctx"), lax.axis_index("head")
    place = lax.rem(ctx, heads)
    base = ctx - place
    team = [(dc, dg) for dc in range(heads) for dg in range(head_n) if (dc, dg) != (0, 0)]
    barrier = pltpu.get_barrier_semaphore()
    for dc, dg in team:
        device = (base + lax.rem(place + dc, heads), lax.rem(head + dg, head_n))
        pl.semaphore_signal(barrier, inc=1, device_id=device, device_id_type=MESH)
    pl.semaphore_wait(barrier, len(team))
    own_slot = head * heads + place

    def tokens_of(to_place, to_head):
        return mine.at[pl.ds(pl.multiple_of((to_place * head_n + to_head) * rows, rows), rows), :]

    copies = []
    for n, (dc, dg) in enumerate(team):
        to_place, to_head = lax.rem(place + dc, heads), lax.rem(head + dg, head_n)
        copy = pltpu.make_async_remote_copy(
            src_ref=tokens_of(to_place, to_head), dst_ref=got.at[own_slot], send_sem=send_sem.at[n],
            recv_sem=recv_sem.at[n], device_id=(base + to_place, to_head), device_id_type=MESH)
        copy.start()
        copies.append(copy)
    own = pltpu.make_async_copy(tokens_of(place, head), got.at[own_slot], local_sem)
    own.start()
    for copy in [own] + copies:
        copy.wait()


def exchange(head_n, heads, rows, normed):
    team = heads * head_n
    return pl.pallas_call(
        functools.partial(exchange_kernel, head_n, heads, rows),
        out_shape=jax.ShapeDtypeStruct((team, rows, DK), BF16),
        in_specs=[pl.BlockSpec(memory_space=pltpu.VMEM)],
        out_specs=pl.BlockSpec(memory_space=pltpu.VMEM),
        scratch_shapes=[pltpu.SemaphoreType.DMA, pltpu.SemaphoreType.DMA((team,)), pltpu.SemaphoreType.DMA((team,))],
        compiler_params=pltpu.CompilerParams(collective_id=1, has_side_effects=True),
    )(normed)


def halves(x):
    top = x.astype(BF16)
    return top, (x - top.astype(F32)).astype(BF16)


def dot(a, b, dims):
    return lax.dot_general(a, b, (dims, ((), ())), preferred_element_type=F32)


NN = ((1,), (0,))
NT = ((1,), (1,))
TN = ((0,), (0,))


def dot3(a, b, dims):
    return dot(a[0], b[0], dims) + (dot(a[0], b[1], dims) + dot(a[1], b[0], dims))


def recur_kernel(per_step, proj, beta, out, through, total, carry):
    step = pl.program_id(0)

    @pl.when(step == 0)
    def _():
        r = lax.broadcasted_iota(jnp.int32, (2 * DK, DK), 0)
        c = lax.broadcasted_iota(jnp.int32, (2 * DK, DK), 1)
        carry[...] = (r - DK == c).astype(F32)

    row = lax.broadcasted_iota(jnp.int32, (FACTORS, FACTORS), 0)
    col = lax.broadcasted_iota(jnp.int32, (FACTORS, FACTORS), 1)
    row_t, col_t = row & (BLOCK - 1), col & (BLOCK - 1)
    strict = (row_t > col_t) | ((row_t == col_t) & (row > col))
    apart = row_t ^ col_t
    eye = (row == col).astype(F32)
    causal = lax.broadcasted_iota(jnp.int32, (BLOCK, FACTORS), 0) >= (
        lax.broadcasted_iota(jnp.int32, (BLOCK, FACTORS), 1) & (BLOCK - 1))

    blocks = []
    for b in range(per_step):
        rows = slice(b * BLOCK, (b + 1) * BLOCK)
        piece = lambda n: proj[rows, n * DK:(n + 1) * DK]
        query = piece(0)
        keys = jnp.concatenate([piece(1 + j) for j in range(NF)], axis=0).astype(F32)
        vals = jnp.concatenate([piece(1 + NF + j) for j in range(NF)], axis=0).astype(F32)
        betas = jnp.concatenate([beta[rows, j:j + 1] for j in range(NF)], axis=0)
        unit = keys / jnp.sqrt(jnp.sum(keys * keys, axis=-1, keepdims=True) + EPSILON)
        unit = (unit, halves(unit))
        low = jnp.where(strict, betas * dot3(unit[1], unit[1], NT), 0.0)
        scores = jnp.where(causal, dot(query, unit[1][0], NT) + dot(query, unit[1][1], NT), 0.0)
        right = jnp.concatenate([betas * vals, betas * unit[0]], axis=1)
        blocks.append(dict(query=query, unit=unit, low=low, scores=scores, right=right, rows=rows))
    for k in blocks:
        near = jnp.where(apart == 0, k["low"], 0.0)
        parts = halves(near)
        k["inv"] = eye - near + dot3(parts, parts, NN)
    reach = 1
    while reach < BLOCK:
        for k in blocks:
            cross = jnp.where((apart >= reach) & (apart < 2 * reach), k["low"], 0.0)
            inv = halves(k["inv"])
            k["mid"] = halves(dot3(halves(cross), inv, NN))
            k["inv_parts"] = inv
        for k in blocks:
            k["inv"] = k["inv"] - dot3(k["inv_parts"], k["mid"], NN)
        reach *= 2
    for k in blocks:
        k["solved"] = halves(dot3(halves(k["inv"]), halves(k["right"]), NN))
    for k in blocks:
        k["moves"] = dot3(k["solved"], k["unit"][1], TN)
        k["seen"] = dot3(halves(k["scores"]), k["solved"], NN)
    for k in blocks:
        state = carry[...]
        parts = halves(state)
        reader = halves(k["query"].astype(F32) - k["seen"][:, DK:])
        read = dot3(reader, parts, NT)
        out[k["rows"], :] = k["seen"][:, :DK] + read[:, :DK]
        through[k["rows"], :] = read[:, DK:]
        moved = state - dot3(parts, halves(k["moves"][DK:]), NN)
        carry[:DK, :] = moved[:DK] + k["moves"][:DK]
        carry[DK:, :] = moved[DK:]

    @pl.when(step == pl.num_programs(0) - 1)
    def _():
        total[...] = carry[...]


def recur(projected, betas):
    tokens = projected.shape[0]
    per_step = 4
    span = per_step * BLOCK
    return pl.pallas_call(
        functools.partial(recur_kernel, per_step),
        grid=(tokens // span,),
        in_specs=[
            pl.BlockSpec((span, COLS), lambda i: (i, 0)),
            pl.BlockSpec((span, NF), lambda i: (i, 0)),
        ],
        out_specs=(
            pl.BlockSpec((span, DK), lambda i: (i, 0)),
            pl.BlockSpec((span, DK), lambda i: (i, 0)),
            pl.BlockSpec((2 * DK, DK), lambda i: (0, 0)),
        ),
        out_shape=(
            jax.ShapeDtypeStruct((tokens, DK), F32),
            jax.ShapeDtypeStruct((tokens, DK), F32),
            jax.ShapeDtypeStruct((2 * DK, DK), F32),
        ),
        scratch_shapes=[pltpu.VMEM((2 * DK, DK), F32)],
        compiler_params=pltpu.CompilerParams(vmem_limit_bytes=40 * 1024 * 1024),
    )(projected, betas)


def shards(activations, w_in, w_beta, beta_bias, head_gain, w_out):
    ctx_n, head_n = lax.axis_size("ctx"), lax.axis_size("head")
    heads = head_gain.shape[0] // DK
    width = activations.shape[1]
    rows = activations.shape[0]
    place = lax.rem(lax.axis_index("ctx"), heads)
    w_beta = jnp.pad(w_beta, ((0, 0), (0, DK - w_beta.shape[1])))
    w_all, beta_all, acts_all, out_all = gather_all(ctx_n, head_n, heads, w_in, w_beta, activations, w_out)
    acts = acts_all.reshape(-1, width)
    proj_sum = jnp.dot(acts, w_all.reshape(width, COLS), preferred_element_type=F32)
    projected = proj_sum.astype(BF16)
    logits = jnp.dot(acts, beta_all.reshape(width, DK), preferred_element_type=F32)
    logits = lax.dynamic_slice_in_dim(logits, place * NF, NF, 1)
    bias = lax.dynamic_slice_in_dim(beta_bias, place * NF, NF, 0)
    betas = 2.0 / (1.0 + jnp.exp(-(logits + bias)))
    out, through, total = recur(projected, betas)
    made, passing = total[:DK], total[DK:]
    route = [(i, i + heads) for i in range(ctx_n - heads)]
    entering = lax.ppermute(made, "ctx", route)
    for _ in range(ctx_n // heads - 2):
        leaving = jnp.dot(entering, passing, precision=PRECISE) + made
        entering = lax.ppermute(leaving, "ctx", route)
    attended = out + jnp.einsum("td,ed->te", through, entering, precision=PRECISE)
    gain = lax.dynamic_slice_in_dim(head_gain, place * DK, DK, 0)
    scale = 1.0 / jnp.sqrt(jnp.mean(attended * attended, axis=-1, keepdims=True) + EPSILON)
    normed = (attended * scale * gain).astype(BF16)
    got = exchange(head_n, heads, rows, normed)
    weights = out_all.reshape(-1, width)
    summed = jnp.zeros((rows, width), F32)
    group = HEADS_DEV * DK
    for n in range(got.shape[0] // HEADS_DEV):
        left = jnp.concatenate([got[n * HEADS_DEV + i] for i in range(HEADS_DEV)], axis=1)
        term = jnp.dot(left, weights[n * group:(n + 1) * group], preferred_element_type=F32)
        summed = summed + lax.optimization_barrier(term.astype(BF16)).astype(F32)
    return summed.astype(BF16)


def solution(mesh):
    return jax.shard_map(
        shards,
        mesh=mesh,
        in_specs=(
            P(("ctx", "head"), None),
            P("ctx", "head"),
            P("ctx", "head"),
            P("head"),
            P("head"),
            P("head", None),
        ),
        out_specs=P(("ctx", "head"), None),
        check_vma=False,
    )
```

time: 1140 us -> 308 us (0.27); the launches traced: 1120 us -> 308 us
  other arithmetic: 649 us -> 2.63 us
  Pallas kernels: 0 us -> 268 us
  waiting for transfers between devices: 253 us -> 4.61 us
  matrix products: 111 us -> 25.3 us
  local copies, waits for them, and re-layouts: 41.6 us -> 5.41 us
  starting transfers between devices: 32.1 us -> 1.47 us
  blocking collectives: 23.1 us -> 0 us
  between operations: 13.9 us -> 0.16 us
    another operation x8 -> x0, other arithmetic: 635 us -> none  [block_terms(): jax.scipy.linalg.solve_triangular(system, right_side, lower=True, unit_di...]
    pallas_call x0 -> x3, Pallas kernels: none -> 268 us  [the longest x1 197 us: gather_all(): pl.pallas_call(functools.partial(gather_kernel, ctx_n, head_n, heads), ou...]
    all_gather x2 -> x0, waiting for transfers between devices: 196 us -> none  [the longest x1 196 us: shards(): lax.all_gather(w_in, 'ctx', axis=0, tiled=True)]
    dot_general x41 -> x7, matrix products: 95.3 us -> 25.3 us  [the longest x1 13.7 us: shards(): jnp.dot(acts, w_all.reshape(width, COLS), preferred_element_type=F32)]
    reduce_scatter x1 -> x0, waiting for transfers between devices: 40.8 us -> none  [shards(): lax.psum_scatter(jnp.dot(normed, w_out, preferred_element_type=jnp.float3...]
    ppermute x7 -> x1, starting transfers between devices: 32 us -> 1.47 us  [shards(): entering = lax.ppermute(made, 'ctx', route)]
    all_gather x1 -> x0, blocking collectives: 23.1 us -> none  [shards(): lax.all_gather(w_beta, 'ctx', axis=0, tiled=True)]
    another operation x3 -> x0, matrix products: 15.4 us -> none  [block_terms(): jax.scipy.linalg.solve_triangular(system, right_side, lower=True, unit_di...]
  transfers between devices with their start and end apart: 10 -> 1, of which waited for: 9 -> 1; matrix products, arithmetic and copies ran while one was open for 1% -> 0% of each run, Pallas kernels for 0% -> 0%
where the time goes in v1:
time: 308 us
  Pallas kernels  268 us (87%)
  matrix products  25.3 us (8%)
  local copies, waits for them, and re-layouts  5.41 us (2%)
  waiting for transfers between devices  4.61 us (1%)
    pallas_call x1, Pallas kernels, gather_all(): pl.pallas_call(functools.partial(gather_kernel, ctx_n, head_n, heads), ou...  197 us
    pallas_call x1, Pallas kernels, recur(): pl.pallas_call(functools.partial(recur_kernel, per_step), grid=(tokens //...  54.5 us
    pallas_call x1, Pallas kernels, exchange(): pl.pallas_call(functools.partial(exchange_kernel, head_n, heads, rows), o...  17.1 us
    dot_general x1, matrix products, shards(): jnp.dot(acts, w_all.reshape(width, COLS), preferred_element_type=F32)  13.7 us
    dot_general x4, matrix products, shards(): jnp.dot(left, weights[n * group:(n + 1) * group], preferred_element_type=...  8.15 us
  transfers between devices with their start and end apart: 1, of which 1 were waited for; matrix products, arithmetic and copies ran while one was open for 0% of the time, Pallas kernels for 0%

profile of v1, /device:TPU:21, one launch (start us, length us, event | category | flops | bytes accessed | tf_op | source)
XLA Modules:
  0.0 307.8 jit_solution(15880158026845432837)
XLA Ops:
  0.0 0.8 copy.10
  0.8 0.6 pad.4.w_beta
  1.5 196.5 %shard_map.64 = (bf16[8,256,896]{2,1,0:T(8,128)(2,1)}, bf16[8,256,128]{2,1,0:T(8,128)(2,1)}, bf16[16,128,2048]{2,1,0:T(8,128)(2,1)}, bf16[4,512,2048]{2,1,0:T(8,128)(2,1)}) custom-call(bf16[256,3584]{1,0:T(8,128)(2,1)} %w_in.1, bf16[256,128]{1,0:T(8,128)(2,1)} %pad.4.w_beta, bf16[128,2048]{1,0:T(8,128)(2,1)} %acts.1, bf16[512,2048]{1,0:T(8,128)(2,1)} %w_out.1), custom_call_target="tpu_custom_call" | custom-call | tf_op jit(solution)/shard_map/pallas_call | solution.py:75
  198.0 0.0 copy-start.1
  198.0 0.0 copy-start.2
  198.1 13.7 %convolution_convert_fusion.proj = bf16[2048,896]{1,0:T(8,128)(2,1)} fusion(bf16[2048,2048]{1,0:T(8,128)(2,1)} %bitcast.53, bf16[2048,896]{1,0:T(8,128)(2,1)} %bitcast.55), kind=kOutput, calls=%fused_computation | convolution fusion | flops 7518027776 | bytes 15728640 | tf_op jit(solution)/shard_map/dot_general | solution.py:251
  211.7 0.0 copy-start.3
  211.7 0.0 copy-done.1
  211.8 0.0 copy-done.2
  211.8 2.4 fusion.40
  214.2 0.0 copy-done.3
  214.2 0.1 dynamic_slice.10
  214.3 0.4 add_divide_fusion.beta
  214.6 0.0 copy-start
  214.6 2.0 copy-done
  216.7 54.5 %shard_map.65 = (f32[2048,128]{1,0:T(8,128)S(1)}, f32[2048,128]{1,0:T(8,128)S(1)}, f32[256,128]{1,0:T(8,128)S(1)}) custom-call(bf16[2048,896]{1,0:T(8,128)(2,1)S(1)} %copy-done, f32[2048,3]{1,0:T(8,128)S(1)} %add_divide_fusion.beta), custom_call_target="tpu_custom_call" | custom-call | tf_op jit(solution)/shard_map/pallas_call | solution.py:220
  271.2 1.5 collective-permute-start
  272.7 0.8 dynamic_slice.11
  273.5 4.6 %collective-permute-done = f32[128,128]{1,0:T(8,128)S(1)} collective-permute-done((f32[128,128]{1,0:T(8,128)S(1)}, f32[128,128]{1,0:T(8,128)S(1)}, u32[]{:S(2)}, u32[]{:S(2)}) %collective-permute-start) | collective-permute-done | bytes 65568 | tf_op jit(solution)/shard_map/ppermute | solution.py:260
  278.1 1.1 multiply_reduce_fusion
  279.2 1.1 multiply_convert_fusion.mine
  280.3 17.1 %shard_map.66 = bf16[16,128,128]{2,1,0:T(8,128)(2,1)} custom-call(bf16[2048,128]{1,0:T(8,128)(2,1)} %multiply_convert_fusion.mine), custom_call_target="tpu_custom_call" | custom-call | tf_op jit(solution)/shard_map/pallas_call | solution.py:121
  297.5 1.0 slice_bitcast_fusion.15
  298.5 2.0 convolution_convert_fusion.1
  300.6 2.0 convolution_convert_fusion.2
  302.6 2.0 convolution_convert_fusion.3
  304.7 2.0 convolution_convert_fusion.4
  306.7 1.1 add_convert_fusion
  (2 shorter events, 0.0 us)
Async XLA Ops:
  198.0 13.7 %copy-start.1 = (bf16[16,128,2048]{2,1,0:T(8,128)(2,1)S(1)}, bf16[16,128,2048]{2,1,0:T(8,128)(2,1)}, u32[]{:S(2)}) copy-start(bf16[16,128,2048]{2,1,0:T(8,128)(2,1)} %get-tuple-element.12) | copy-start | bytes 25165828
  198.0 13.7 %copy-start.2 = (bf16[8,256,128]{2,1,0:T(8,128)(2,1)S(1)}, bf16[8,256,128]{2,1,0:T(8,128)(2,1)}, u32[]{:S(2)}) copy-start(bf16[8,256,128]{2,1,0:T(8,128)(2,1)} %get-tuple-element.14) | copy-start | bytes 1572868
  211.7 2.4 copy-start.3
  214.6 2.0 copy-start
  271.2 6.9 %collective-permute-start = (f32[128,128]{1,0:T(8,128)S(1)}, f32[128,128]{1,0:T(8,128)S(1)}, u32[]{:S(2)}, u32[]{:S(2)}) collective-permute-start(f32[128,128]{1,0:T(8,128)S(1)} %slice.75), channel_id=1, source_target_pairs={{0,16},{4,20},{8,24},{12,28},{1,17},{5,21},{9,25},{13,29},{2,18},{... | collective-permute-start | bytes 196616 | tf_op jit(solution)/shard_map/ppermute | solution.py:260

commit v2 on v1

--- a/solution.py
+++ b/solution.py
@@ -25,38 +25,76 @@
     ctx, head = lax.axis_index("ctx"), lax.axis_index("head")
     place = lax.rem(ctx, heads)
     base = ctx - place
-    team = [(dc, dg) for dc in range(heads) for dg in range(head_n) if (dc, dg) != (0, 0)]
-
-    def teammate(dc, dg):
-        return (base + lax.rem(place + dc, heads), lax.rem(head + dg, head_n))
+    pairs = head_n // 2
+    core = lax.rem(head, 2)
+    pair = head // 2
+    sibling = (ctx, pair * 2 + (1 - core))
+
+    def across(dx):
+        return (ctx, lax.rem(pair + dx, pairs) * 2 + core)
+
+    def teammate(dc):
+        return (base + lax.rem(place + dc, heads), head)
 
     barrier = pltpu.get_barrier_semaphore()
     for off in range(1, ctx_n):
         pl.semaphore_signal(barrier, inc=1, device_id=(lax.rem(ctx + off, ctx_n), head), device_id_type=MESH)
-    for dc, dg in team:
-        pl.semaphore_signal(barrier, inc=1, device_id=teammate(dc, dg), device_id_type=MESH)
-    pl.semaphore_wait(barrier, ctx_n - 1 + len(team))
+    for dx in range(1, pairs):
+        pl.semaphore_signal(barrier, inc=1, device_id=across(dx), device_id_type=MESH)
+    pl.semaphore_signal(barrier, inc=1, device_id=sibling, device_id_type=MESH)
+    pl.semaphore_wait(barrier, ctx_n - 1 + pairs)
 
     def columns(of):
         return w_in.at[:, pl.ds(pl.multiple_of(lax.rem(of, heads) * COLS, DK), COLS)]
 
-    copies = []
+    started, finish = [], []
 
     def send(src, dst, ssem, rsem, device):
         copy = pltpu.make_async_remote_copy(src_ref=src, dst_ref=dst, send_sem=ssem, recv_sem=rsem,
                                             device_id=device, device_id_type=MESH)
         copy.start()
-        copies.append(copy)
-
+        started.append(copy)
+        return copy
+
+    def head_at(dx, dcore):
+        return lax.rem(pair + pairs - dx, pairs) * 2 + lax.rem(core + dcore, 2)
+
+    def act_slot(dc, dx, dcore):
+        return acts_all.at[lax.rem(place + heads - dc, heads) * head_n + head_at(dx, dcore)]
+
+    def index_of(dc, dx, dcore):
+        return (dc * pairs + dx) * 2 + dcore
+
+    def send_acts(src, came, lands, device):
+        send(src, act_slot(*came), a_send.at[index_of(*lands)], a_recv.at[index_of(*lands)], device)
+
+    def wait_acts(*came):
+        n = index_of(*came)
+        pltpu.make_async_remote_copy(src_ref=acts, dst_ref=act_slot(*came), send_sem=a_send.at[n],
+                                     recv_sem=a_recv.at[n], device_id=sibling, device_id_type=MESH).wait_recv()
+
+    def send_out(src, came, n, device):
+        send(src, out_all.at[head_at(came, 0)], o_send.at[n], o_recv.at[n], device)
+
+    def wait_out(dx, dcore):
+        n = dx * 2 + dcore
+        pltpu.make_async_remote_copy(src_ref=w_out, dst_ref=out_all.at[head_at(dx, dcore)], send_sem=o_send.at[n],
+                                     recv_sem=o_recv.at[n], device_id=sibling, device_id_type=MESH).wait_recv()
+
+    mine = (0, 0, 0)
+    for dc in range(1, heads):
+        send_acts(acts, mine, (dc, 0, 0), teammate(dc))
+    for dx in range(1, pairs):
+        send_acts(acts, mine, (0, dx, 0), across(dx))
+    send_acts(acts, mine, (0, 0, 1), sibling)
     order = sorted(range(1, ctx_n), key=lambda off: -min(off, ctx_n - off))
     for off in order:
         to = lax.rem(ctx + off, ctx_n)
-        send(columns(to), w_all.at[ctx], w_send.at[off], w_recv.at[off], (to, head))
-        send(w_beta, beta_all.at[ctx], b_send.at[off], b_recv.at[off], (to, head))
-    for n, (dc, dg) in enumerate(team):
-        send(acts, acts_all.at[place * head_n + head], a_send.at[n], a_recv.at[n], teammate(dc, dg))
-    for off in range(1, head_n):
-        send(w_out, out_all.at[head], o_send.at[off], o_recv.at[off], (ctx, lax.rem(head + off, head_n)))
+        finish.append(send(columns(to), w_all.at[ctx], w_send.at[off], w_recv.at[off], (to, head)))
+        finish.append(send(w_beta, beta_all.at[ctx], b_send.at[off], b_recv.at[off], (to, head)))
+    for dx in range(1, pairs):
+        send_out(w_out, 0, dx * 2, across(dx))
+    send_out(w_out, 0, 1, sibling)
     own = [
         pltpu.make_async_copy(columns(ctx), w_all.at[ctx], local_sem.at[0]),
         pltpu.make_async_copy(w_beta, beta_all.at[ctx], local_sem.at[1]),
@@ -65,7 +103,30 @@
     ]
     for copy in own:
         copy.start()
-    for copy in own + copies:
+    for dc in range(1, heads):
+        came = (dc, 0, 0)
+        wait_acts(*came)
+        for dx in range(1, pairs):
+            send_acts(act_slot(*came), came, (dc, dx, 0), across(dx))
+        send_acts(act_slot(*came), came, (dc, 0, 1), sibling)
+    for dc in range(heads):
+        for dx in range(1, pairs):
+            came = (dc, dx, 0)
+            wait_acts(*came)
+            send_acts(act_slot(*came), came, (dc, dx, 1), sibling)
+    for dx in range(1, pairs):
+        wait_out(dx, 0)
+        send_out(out_all.at[head_at(dx, 0)], dx, dx * 2 + 1, sibling)
+    for dc in range(heads):
+        for dx in range(pairs):
+            wait_acts(dc, dx, 1)
+    for dx in range(pairs):
+        wait_out(dx, 1)
+    for copy in finish:
+        copy.wait_recv()
+    for copy in started:
+        copy.wait_send()
+    for copy in own:
         copy.wait()
 
 
@@ -87,11 +148,13 @@
     )(w_in, w_beta, acts, w_out)
 
 
-def exchange_kernel(head_n, heads, rows, mine, got, local_sem, send_sem, recv_sem):
+def exchange_kernel(head_n, heads, rows, mine, weights, mixed, got, held, local_sem, held_sem, send_sem, recv_sem):
     ctx, head = lax.axis_index("ctx"), lax.axis_index("head")
     place = lax.rem(ctx, heads)
     base = ctx - place
     team = [(dc, dg) for dc in range(heads) for dg in range(head_n) if (dc, dg) != (0, 0)]
+    fetch = pltpu.make_async_copy(weights, held, held_sem)
+    fetch.start()
     barrier = pltpu.get_barrier_semaphore()
     for dc, dg in team:
         device = (base + lax.rem(place + dc, heads), lax.rem(head + dg, head_n))
@@ -112,20 +175,38 @@
         copies.append(copy)
     own = pltpu.make_async_copy(tokens_of(place, head), got.at[own_slot], local_sem)
     own.start()
-    for copy in [own] + copies:
+    for copy in [own, fetch] + copies:
         copy.wait()
-
-
-def exchange(head_n, heads, rows, normed):
+    group = HEADS_DEV * DK
+    lefts = [
+        jnp.concatenate([got[n * HEADS_DEV + i] for i in range(HEADS_DEV)], axis=1)
+        for n in range(heads * head_n // HEADS_DEV)
+    ]
+    tile = 512
+    for at in range(0, mixed.shape[1], tile):
+        summed = None
+        for n, left in enumerate(lefts):
+            term = jnp.dot(left, held[n * group:(n + 1) * group, at:at + tile], preferred_element_type=F32)
+            term = term.astype(BF16).astype(F32)
+            summed = term if summed is None else summed + term
+        mixed[:, at:at + tile] = summed.astype(BF16)
+
+
+def exchange(head_n, heads, rows, normed, weights):
     team = heads * head_n
+    dma = pltpu.SemaphoreType.DMA
     return pl.pallas_call(
         functools.partial(exchange_kernel, head_n, heads, rows),
-        out_shape=jax.ShapeDtypeStruct((team, rows, DK), BF16),
-        in_specs=[pl.BlockSpec(memory_space=pltpu.VMEM)],
+        out_shape=jax.ShapeDtypeStruct((rows, weights.shape[1]), BF16),
+        in_specs=[pl.BlockSpec(memory_space=pltpu.VMEM), pl.BlockSpec(memory_space=pl.ANY)],
         out_specs=pl.BlockSpec(memory_space=pltpu.VMEM),
-        scratch_shapes=[pltpu.SemaphoreType.DMA, pltpu.SemaphoreType.DMA((team,)), pltpu.SemaphoreType.DMA((team,))],
-        compiler_params=pltpu.CompilerParams(collective_id=1, has_side_effects=True),
-    )(normed)
+        scratch_shapes=[
+            pltpu.VMEM((team, rows, DK), BF16),
+            pltpu.VMEM(weights.shape, BF16),
+            dma, dma, dma((team,)), dma((team,)),
+        ],
+        compiler_params=pltpu.CompilerParams(collective_id=1, has_side_effects=True, vmem_limit_bytes=40 * 1024 * 1024),
+    )(normed, weights)
 
 
 def halves(x):
@@ -265,15 +346,7 @@
     gain = lax.dynamic_slice_in_dim(head_gain, place * DK, DK, 0)
     scale = 1.0 / jnp.sqrt(jnp.mean(attended * attended, axis=-1, keepdims=True) + EPSILON)
     normed = (attended * scale * gain).astype(BF16)
-    got = exchange(head_n, heads, rows, normed)
-    weights = out_all.reshape(-1, width)
-    summed = jnp.zeros((rows, width), F32)
-    group = HEADS_DEV * DK
-    for n in range(got.shape[0] // HEADS_DEV):
-        left = jnp.concatenate([got[n * HEADS_DEV + i] for i in range(HEADS_DEV)], axis=1)
-        term = jnp.dot(left, weights[n * group:(n + 1) * group], preferred_element_type=F32)
-        summed = summed + lax.optimization_barrier(term.astype(BF16)).astype(F32)
-    return summed.astype(BF16)
+    return exchange(head_n, heads, rows, normed, out_all.reshape(-1, width))
 
 
 def solution(mesh):

time: 308 us -> 202 us (0.66)
  Pallas kernels: 268 us -> 170 us
  matrix products: 25.3 us -> 17.2 us
  local copies, waits for them, and re-layouts: 5.41 us -> 8.53 us
    pallas_call x1, Pallas kernels: 197 us -> 101 us  [gather_all(): pl.pallas_call(functools.partial(gather_kernel, ctx_n, head_n, heads), ou...]
    dot_general x4 -> x0, matrix products: 8.15 us -> none  [shards(): jnp.dot(left, weights[n * group:(n + 1) * group], preferred_element_type=...]
    unnamed x9 -> x12, local copies, waits for them, and re-layouts: 2.88 us -> 7.05 us
where the time goes in v2:
time: 202 us
  Pallas kernels  170 us (84%)
  matrix products  17.2 us (9%)
  local copies, waits for them, and re-layouts  8.53 us (4%)
  waiting for transfers between devices  3.76 us (2%)
    pallas_call x1, Pallas kernels, gather_all(): pl.pallas_call(functools.partial(gather_kernel, ctx_n, head_n, heads), ou...  101 us
    pallas_call x1, Pallas kernels, recur(): pl.pallas_call(functools.partial(recur_kernel, per_step), grid=(tokens //...  54.5 us
    pallas_call x1, Pallas kernels, exchange(): pl.pallas_call(functools.partial(exchange_kernel, head_n, heads, rows), o...  14.7 us
    dot_general x1, matrix products, shards(): jnp.dot(acts, w_all.reshape(width, COLS), preferred_element_type=F32)  13.7 us
    unnamed x12, local copies, waits for them, and re-layouts  7.05 us
  transfers between devices with their start and end apart: 1, of which 1 were waited for; matrix products, arithmetic and copies ran while one was open for 0% of the time, Pallas kernels for 0%

profile of v2, /device:TPU:21, one launch (start us, length us, event | category | flops | bytes accessed | tf_op | source)
XLA Modules:
  0.0 201.6 jit_solution(2443787452251095859)
XLA Ops:
  0.0 0.8 copy.10
  0.8 0.6 pad.4.w_beta
  1.5 100.5 %shard_map.64 = (bf16[8,256,896]{2,1,0:T(8,128)(2,1)}, bf16[8,256,128]{2,1,0:T(8,128)(2,1)}, bf16[16,128,2048]{2,1,0:T(8,128)(2,1)}, bf16[4,512,2048]{2,1,0:T(8,128)(2,1)}) custom-call(bf16[256,3584]{1,0:T(8,128)(2,1)} %w_in.1, bf16[256,128]{1,0:T(8,128)(2,1)} %pad.4.w_beta, bf16[128,2048]{1,0:T(8,128)(2,1)} %acts.1, bf16[512,2048]{1,0:T(8,128)(2,1)} %w_out.1), custom_call_target="tpu_custom_call" | custom-call | tf_op jit(solution)/shard_map/pallas_call | solution.py:136
  102.0 0.0 copy-start.2
  102.0 0.0 copy-start.3
  102.0 13.7 %convolution_convert_fusion.proj = bf16[2048,896]{1,0:T(8,128)(2,1)} fusion(bf16[2048,2048]{1,0:T(8,128)(2,1)} %bitcast.11, bf16[2048,896]{1,0:T(8,128)(2,1)} %bitcast.13), kind=kOutput, calls=%fused_computation | convolution fusion | flops 7518027776 | bytes 15728640 | tf_op jit(solution)/shard_map/dot_general | solution.py:332
  115.7 0.0 copy-start.4
  115.7 0.0 copy-done.2
  115.7 0.0 copy-done.3
  115.7 2.4 %fusion = f32[2048,128]{1,0:T(8,128)S(1)} fusion(bf16[2048,2048]{1,0:T(8,128)(2,1)S(1)} %bitcast.12, bf16[2048,128]{1,0:T(8,128)(2,1)S(1)} %bitcast.14), kind=kOutput, calls=%fused_computation.6 | convolution fusion | flops 1073741824 | bytes 9961472 | tf_op jit(solution)/shard_map/dot_general | solution.py:334
  118.1 0.0 copy-done.4
  118.1 0.1 dynamic_slice.10
  118.2 0.4 add_divide_fusion.beta
  118.6 0.0 copy-start.1
  118.6 2.0 %copy-done.1 = bf16[2048,896]{1,0:T(8,128)(2,1)S(1)} copy-done((bf16[2048,896]{1,0:T(8,128)(2,1)S(1)}, bf16[2048,896]{1,0:T(8,128)(2,1)}, u32[]{:S(2)}) %copy-start.1) | copy-done | bytes 3670040
  120.6 54.5 %shard_map.65 = (f32[2048,128]{1,0:T(8,128)S(1)}, f32[2048,128]{1,0:T(8,128)S(1)}, f32[256,128]{1,0:T(8,128)S(1)}) custom-call(bf16[2048,896]{1,0:T(8,128)(2,1)S(1)} %copy-done.1, f32[2048,3]{1,0:T(8,128)S(1)} %add_divide_fusion.beta), custom_call_target="tpu_custom_call" | custom-call | tf_op jit(solution)/shard_map/pallas_call | solution.py:301
  175.2 1.5 collective-permute-start
  176.7 0.8 dynamic_slice.11
  177.4 3.8 %collective-permute-done = f32[128,128]{1,0:T(8,128)S(1)} collective-permute-done((f32[128,128]{1,0:T(8,128)S(1)}, f32[128,128]{1,0:T(8,128)S(1)}, u32[]{:S(2)}, u32[]{:S(2)}) %collective-permute-start) | collective-permute-done | bytes 65568 | tf_op jit(solution)/shard_map/ppermute | solution.py:341
  181.2 1.1 multiply_reduce_fusion
  182.3 0.3 multiply_convert_fusion.mine
  182.7 0.0 copy-start
  182.7 3.4 %copy-done = bf16[4,512,2048]{2,1,0:T(8,128)(2,1)S(1)} copy-done((bf16[4,512,2048]{2,1,0:T(8,128)(2,1)S(1)}, bf16[4,512,2048]{2,1,0:T(8,128)(2,1)}, u32[]{:S(2)}) %copy-start) | copy-done | bytes 8388632
  186.0 14.7 %shard_map.66 = bf16[128,2048]{1,0:T(8,128)(2,1)S(1)} custom-call(bf16[2048,128]{1,0:T(8,128)(2,1)S(1)} %multiply_convert_fusion.mine, bf16[2048,2048]{1,0:T(8,128)(2,1)S(1)} %bitcast.10), custom_call_target="tpu_custom_call" | custom-call | tf_op jit(solution)/shard_map/pallas_call | solution.py:198
  200.8 0.8 copy.17
  (2 shorter events, 0.0 us)
Async XLA Ops:
  102.0 13.7 %copy-start.2 = (bf16[16,128,2048]{2,1,0:T(8,128)(2,1)S(1)}, bf16[16,128,2048]{2,1,0:T(8,128)(2,1)}, u32[]{:S(2)}) copy-start(bf16[16,128,2048]{2,1,0:T(8,128)(2,1)} %get-tuple-element.12) | copy-start | bytes 25165828
  102.0 13.7 %copy-start.3 = (bf16[8,256,128]{2,1,0:T(8,128)(2,1)S(1)}, bf16[8,256,128]{2,1,0:T(8,128)(2,1)}, u32[]{:S(2)}) copy-start(bf16[8,256,128]{2,1,0:T(8,128)(2,1)} %get-tuple-element.14) | copy-start | bytes 1572868
  115.7 2.4 %copy-start.4 = (f32[12]{0:T(128)S(1)}, f32[12]{0:T(128)}, u32[]{:S(2)}) copy-start(f32[12]{0:T(128)} %param.9) | copy-start | bytes 148
  118.6 2.0 %copy-start.1 = (bf16[2048,896]{1,0:T(8,128)(2,1)S(1)}, bf16[2048,896]{1,0:T(8,128)(2,1)}, u32[]{:S(2)}) copy-start(bf16[2048,896]{1,0:T(8,128)(2,1)} %convolution_convert_fusion.proj) | copy-start | bytes 11010052
  175.2 6.0 %collective-permute-start = (f32[128,128]{1,0:T(8,128)S(1)}, f32[128,128]{1,0:T(8,128)S(1)}, u32[]{:S(2)}, u32[]{:S(2)}) collective-permute-start(f32[128,128]{1,0:T(8,128)S(1)} %slice.3), channel_id=1, source_target_pairs={{0,16},{4,20},{8,24},{12,28},{1,17},{5,21},{9,25},{13,29},{2,18},{... | collective-permute-start | bytes 196616 | tf_op jit(solution)/shard_map/ppermute | solution.py:341
  182.7 3.4 %copy-start = (bf16[4,512,2048]{2,1,0:T(8,128)(2,1)S(1)}, bf16[4,512,2048]{2,1,0:T(8,128)(2,1)}, u32[]{:S(2)}) copy-start(bf16[4,512,2048]{2,1,0:T(8,128)(2,1)} %get-tuple-element.18) | copy-start | bytes 25165828

commit v3 on v2

--- a/solution.py
+++ b/solution.py
@@ -205,7 +205,7 @@
             pltpu.VMEM(weights.shape, BF16),
             dma, dma, dma((team,)), dma((team,)),
         ],
-        compiler_params=pltpu.CompilerParams(collective_id=1, has_side_effects=True, vmem_limit_bytes=40 * 1024 * 1024),
+        compiler_params=pltpu.CompilerParams(collective_id=1, has_side_effects=True, vmem_limit_bytes=56 * 1024 * 1024),
     )(normed, weights)
 
 
@@ -227,8 +227,14 @@
     return dot(a[0], b[0], dims) + (dot(a[0], b[1], dims) + dot(a[1], b[0], dims))
 
 
-def recur_kernel(per_step, proj, beta, out, through, total, carry):
+def recur_kernel(per_step, heads, acts, w_head, w_beta, bias, out, through, total, carry):
     step = pl.program_id(0)
+    first = lax.rem(lax.axis_index("ctx"), heads) * NF
+    proj = jnp.dot(acts[...], w_head[...], preferred_element_type=F32).astype(BF16)
+    logits = jnp.dot(acts[...], w_beta[...], preferred_element_type=F32) + bias[...]
+    gates = 2.0 / (1.0 + jnp.exp(-logits))
+    lane = lax.broadcasted_iota(jnp.int32, gates.shape, 1)
+    beta = [jnp.sum(jnp.where(lane == first + j, gates, 0.0), axis=1, keepdims=True) for j in range(NF)]
 
     @pl.when(step == 0)
     def _():
@@ -252,7 +258,7 @@
         query = piece(0)
         keys = jnp.concatenate([piece(1 + j) for j in range(NF)], axis=0).astype(F32)
         vals = jnp.concatenate([piece(1 + NF + j) for j in range(NF)], axis=0).astype(F32)
-        betas = jnp.concatenate([beta[rows, j:j + 1] for j in range(NF)], axis=0)
+        betas = jnp.concatenate([beta[j][rows] for j in range(NF)], axis=0)
         unit = keys / jnp.sqrt(jnp.sum(keys * keys, axis=-1, keepdims=True) + EPSILON)
         unit = (unit, halves(unit))
         low = jnp.where(strict, betas * dot3(unit[1], unit[1], NT), 0.0)
@@ -261,18 +267,29 @@
         blocks.append(dict(query=query, unit=unit, low=low, scores=scores, right=right, rows=rows))
     for k in blocks:
         near = jnp.where(apart == 0, k["low"], 0.0)
-        parts = halves(near)
-        k["inv"] = eye - near + dot3(parts, parts, NN)
+        parts = near.astype(BF16)
+        k["inv"] = eye - near + dot(parts, parts, NN)
     reach = 1
     while reach < BLOCK:
         for k in blocks:
-            cross = jnp.where((apart >= reach) & (apart < 2 * reach), k["low"], 0.0)
-            inv = halves(k["inv"])
-            k["mid"] = halves(dot3(halves(cross), inv, NN))
-            k["inv_parts"] = inv
+            cross = jnp.where((apart >= reach) & (apart < 2 * reach), k["low"], 0.0).astype(BF16)
+            k["inv_parts"] = k["inv"].astype(BF16)
+            k["mid"] = dot(cross, k["inv_parts"], NN).astype(BF16)
         for k in blocks:
-            k["inv"] = k["inv"] - dot3(k["inv_parts"], k["mid"], NN)
+            k["inv"] = k["inv"] - dot(k["inv_parts"], k["mid"], NN)
         reach *= 2
+    for k in blocks:
+        k["low_parts"] = halves(k["low"])
+        k["rough"] = k["inv"].astype(BF16)
+    for k in blocks:
+        rough = k["rough"]
+        left = (eye - rough.astype(F32)) - (dot(k["low_parts"][0], rough, NN) + dot(k["low_parts"][1], rough, NN))
+        k["left"] = left.astype(BF16)
+    for k in blocks:
+        k["inv"] = k["rough"].astype(F32) + dot(k["rough"], k["left"], NN)
+    for k in blocks:
+        left = (eye - k["inv"]) - dot3(k["low_parts"], halves(k["inv"]), NN)
+        k["inv"] = k["inv"] + dot(k["rough"], left.astype(BF16), NN)
     for k in blocks:
         k["solved"] = halves(dot3(halves(k["inv"]), halves(k["right"]), NN))
     for k in blocks:
@@ -294,16 +311,18 @@
         total[...] = carry[...]
 
 
-def recur(projected, betas):
-    tokens = projected.shape[0]
-    per_step = 4
+def recur(heads, acts, w_head, w_beta, bias):
+    tokens, width = acts.shape
+    per_step = 8
     span = per_step * BLOCK
     return pl.pallas_call(
-        functools.partial(recur_kernel, per_step),
+        functools.partial(recur_kernel, per_step, heads),
         grid=(tokens // span,),
         in_specs=[
-            pl.BlockSpec((span, COLS), lambda i: (i, 0)),
-            pl.BlockSpec((span, NF), lambda i: (i, 0)),
+            pl.BlockSpec((span, width), lambda i: (i, 0)),
+            pl.BlockSpec((width, COLS), lambda i: (0, 0)),
+            pl.BlockSpec((width, DK), lambda i: (0, 0)),
+            pl.BlockSpec((1, DK), lambda i: (0, 0)),
         ],
         out_specs=(
             pl.BlockSpec((span, DK), lambda i: (i, 0)),
@@ -316,8 +335,8 @@
             jax.ShapeDtypeStruct((2 * DK, DK), F32),
         ),
         scratch_shapes=[pltpu.VMEM((2 * DK, DK), F32)],
-        compiler_params=pltpu.CompilerParams(vmem_limit_bytes=40 * 1024 * 1024),
-    )(projected, betas)
+        compiler_params=pltpu.CompilerParams(vmem_limit_bytes=56 * 1024 * 1024),
+    )(acts, w_head, w_beta, bias)
 
 
 def shards(activations, w_in, w_beta, beta_bias, head_gain, w_out):
@@ -329,13 +348,8 @@
     w_beta = jnp.pad(w_beta, ((0, 0), (0, DK - w_beta.shape[1])))
     w_all, beta_all, acts_all, out_all = gather_all(ctx_n, head_n, heads, w_in, w_beta, activations, w_out)
     acts = acts_all.reshape(-1, width)
-    proj_sum = jnp.dot(acts, w_all.reshape(width, COLS), preferred_element_type=F32)
-    projected = proj_sum.astype(BF16)
-    logits = jnp.dot(acts, beta_all.reshape(width, DK), preferred_element_type=F32)
-    logits = lax.dynamic_slice_in_dim(logits, place * NF, NF, 1)
-    bias = lax.dynamic_slice_in_dim(beta_bias, place * NF, NF, 0)
-    betas = 2.0 / (1.0 + jnp.exp(-(logits + bias)))
-    out, through, total = recur(projected, betas)
+    bias = jnp.pad(beta_bias, (0, DK - beta_bias.shape[0])).reshape(1, DK)
+    out, through, total = recur(heads, acts, w_all.reshape(width, COLS), beta_all.reshape(width, DK), bias)
     made, passing = total[:DK], total[DK:]
     route = [(i, i + heads) for i in range(ctx_n - heads)]
     entering = lax.ppermute(made, "ctx", route)

time: 202 us -> 197 us (0.975)
  matrix products: 17.2 us -> 2.62 us
  Pallas kernels: 170 us -> 181 us
  local copies, waits for them, and re-layouts: 8.53 us -> 6.16 us
    dot_general x2 -> x0, matrix products: 16.1 us -> none  [the longest x1 13.7 us: shards(): jnp.dot(acts, w_all.reshape(width, COLS), preferred_element_type=F32)]
    pallas_call x1, Pallas kernels: 54.5 us -> 64.9 us  [recur(): pl.pallas_call(functools.partial(recur_kernel, per_step, heads), grid=(to...]
    unnamed x12 -> x2, local copies, waits for them, and re-layouts: 7.05 us -> 2.71 us
where the time goes in v3:
time: 197 us
  Pallas kernels  181 us (92%)
  local copies, waits for them, and re-layouts  6.16 us (3%)
  waiting for transfers between devices  3.94 us (2%)
  matrix products  2.62 us (1%)
    pallas_call x1, Pallas kernels, gather_all(): pl.pallas_call(functools.partial(gather_kernel, ctx_n, head_n, heads), ou...  101 us
    pallas_call x1, Pallas kernels, recur(): pl.pallas_call(functools.partial(recur_kernel, per_step, heads), grid=(to...  64.9 us
    pallas_call x1, Pallas kernels, exchange(): pl.pallas_call(functools.partial(exchange_kernel, head_n, heads, rows), o...  16 us
  transfers between devices with their start and end apart: 1, of which 1 were waited for; matrix products, arithmetic and copies ran while one was open for 0% of the time, Pallas kernels for 0%

profile of v3, /device:TPU:21, one launch (start us, length us, event | category | flops | bytes accessed | tf_op | source)
XLA Modules:
  0.0 196.6 jit_solution(8612873404320687286)
XLA Ops:
  0.0 0.8 copy.7
  0.8 1.2 pad_bitcast_fusion.bias
  2.0 0.6 pad.8.w_beta
  2.7 100.5 %shard_map.64 = (bf16[8,256,896]{2,1,0:T(8,128)(2,1)}, bf16[8,256,128]{2,1,0:T(8,128)(2,1)}, bf16[16,128,2048]{2,1,0:T(8,128)(2,1)}, bf16[4,512,2048]{2,1,0:T(8,128)(2,1)}) custom-call(bf16[256,3584]{1,0:T(8,128)(2,1)} %w_in.1, bf16[256,128]{1,0:T(8,128)(2,1)} %pad.8.w_beta, bf16[128,2048]{1,0:T(8,128)(2,1)} %acts.1, bf16[512,2048]{1,0:T(8,128)(2,1)} %w_out.1), custom_call_target="tpu_custom_call" | custom-call | tf_op jit(solution)/shard_map/pallas_call | solution.py:136
  103.2 64.9 %shard_map.65 = (f32[2048,128]{1,0:T(8,128)}, f32[2048,128]{1,0:T(8,128)}, f32[256,128]{1,0:T(8,128)}) custom-call(bf16[2048,2048]{1,0:T(8,128)(2,1)} %bitcast.9, bf16[2048,896]{1,0:T(8,128)(2,1)} %bitcast.10, bf16[2048,128]{1,0:T(8,128)(2,1)} %bitcast.11, f32[1,128]{1,0:T(1,128)} %pad_bitcast_fusion.bias), custom_call_target="tpu_custom_call" | custom-call | tf_op jit(solution)/shard_map/pallas_call | solution.py:318
  168.1 0.8 slice.3
  169.0 1.3 collective-permute-start
  170.3 0.8 dynamic_slice.3
  171.0 3.9 %collective-permute-done = f32[128,128]{1,0:T(8,128)S(1)} collective-permute-done((f32[128,128]{1,0:T(8,128)S(1)}, f32[128,128]{1,0:T(8,128)S(1)}, u32[]{:S(2)}, u32[]{:S(2)}) %collective-permute-start) | collective-permute-done | bytes 65568 | tf_op jit(solution)/shard_map/ppermute | solution.py:355
  174.9 2.6 %multiply_reduce_fusion = (f32[2048]{0:T(1024)S(1)}, f32[2048,128]{1,0:T(8,128)S(1)}) fusion(f32[2048,128]{1,0:T(8,128)} %get-tuple-element.15, f32[2048,128]{1,0:T(8,128)} %get-tuple-element.16, f32[128,128]{1,0:T(8,128)S(1)} %collective-permute-done), kind=kOutput, calls=%fused_computation.2 | convolution fusion | flops 403437568 | bytes 3219456 | tf_op jit(solution)/shard_map/td,ed->te/dot_general | solution.py:359
  177.6 1.1 multiply_convert_fusion.mine
  178.7 16.0 %shard_map.66 = bf16[128,2048]{1,0:T(8,128)(2,1)} custom-call(bf16[2048,128]{1,0:T(8,128)(2,1)} %multiply_convert_fusion.mine, bf16[2048,2048]{1,0:T(8,128)(2,1)} %bitcast.8), custom_call_target="tpu_custom_call" | custom-call | tf_op jit(solution)/shard_map/pallas_call | solution.py:198
  194.7 1.9 copy.11
  (1 shorter events, 0.0 us)
Async XLA Ops:
  169.0 6.0 %collective-permute-start = (f32[128,128]{1,0:T(8,128)S(1)}, f32[128,128]{1,0:T(8,128)S(1)}, u32[]{:S(2)}, u32[]{:S(2)}) collective-permute-start(f32[128,128]{1,0:T(8,128)S(1)} %slice.3), channel_id=1, source_target_pairs={{0,16},{4,20},{8,24},{12,28},{1,17},{5,21},{9,25},{13,29},{2,18},{... | collective-permute-start | bytes 196616 | tf_op jit(solution)/shard_map/ppermute | solution.py:355

commit v4 on v3

--- a/solution.py
+++ b/solution.py
@@ -284,12 +284,10 @@
     for k in blocks:
         rough = k["rough"]
         left = (eye - rough.astype(F32)) - (dot(k["low_parts"][0], rough, NN) + dot(k["low_parts"][1], rough, NN))
-        k["left"] = left.astype(BF16)
-    for k in blocks:
-        k["inv"] = k["rough"].astype(F32) + dot(k["rough"], k["left"], NN)
-    for k in blocks:
-        left = (eye - k["inv"]) - dot3(k["low_parts"], halves(k["inv"]), NN)
-        k["inv"] = k["inv"] + dot(k["rough"], left.astype(BF16), NN)
+        near = left.astype(BF16)
+        k["left"] = halves(left + dot(near, near, NN))
+    for k in blocks:
+        k["inv"] = k["rough"].astype(F32) + (dot(k["rough"], k["left"][0], NN) + dot(k["rough"], k["left"][1], NN))
     for k in blocks:
         k["solved"] = halves(dot3(halves(k["inv"]), halves(k["right"]), NN))
     for k in blocks:

time: 197 us -> 195 us (0.990)
  Pallas kernels: 181 us -> 179 us
    pallas_call x1, Pallas kernels: 64.9 us -> 62.5 us  [recur(): pl.pallas_call(functools.partial(recur_kernel, per_step, heads), grid=(to...]
where the time goes in v4:
time: 195 us; the launch traced here: 194 us
  Pallas kernels  179 us (92%)
  local copies, waits for them, and re-layouts  6.16 us (3%)
  waiting for transfers between devices  3.76 us (2%)
  matrix products  2.62 us (1%)
    pallas_call x1, Pallas kernels, gather_all(): pl.pallas_call(functools.partial(gather_kernel, ctx_n, head_n, heads), ou...  101 us
    pallas_call x1, Pallas kernels, recur(): pl.pallas_call(functools.partial(recur_kernel, per_step, heads), grid=(to...  62.5 us
    pallas_call x1, Pallas kernels, exchange(): pl.pallas_call(functools.partial(exchange_kernel, head_n, heads, rows), o...  16 us
  transfers between devices with their start and end apart: 1, of which 1 were waited for; matrix products, arithmetic and copies ran while one was open for 0% of the time, Pallas kernels for 0%

profile of v4, /device:TPU:21, one launch (start us, length us, event | category | flops | bytes accessed | tf_op | source)
XLA Modules:
  0.0 194.2 jit_solution(18298564559199964320)
XLA Ops:
  0.0 0.8 copy.7
  0.8 1.2 pad_bitcast_fusion.bias
  2.0 0.6 pad.8.w_beta
  2.7 100.5 %shard_map.64 = (bf16[8,256,896]{2,1,0:T(8,128)(2,1)}, bf16[8,256,128]{2,1,0:T(8,128)(2,1)}, bf16[16,128,2048]{2,1,0:T(8,128)(2,1)}, bf16[4,512,2048]{2,1,0:T(8,128)(2,1)}) custom-call(bf16[256,3584]{1,0:T(8,128)(2,1)} %w_in.1, bf16[256,128]{1,0:T(8,128)(2,1)} %pad.8.w_beta, bf16[128,2048]{1,0:T(8,128)(2,1)} %acts.1, bf16[512,2048]{1,0:T(8,128)(2,1)} %w_out.1), custom_call_target="tpu_custom_call" | custom-call | tf_op jit(solution)/shard_map/pallas_call | solution.py:136
  103.2 62.5 %shard_map.65 = (f32[2048,128]{1,0:T(8,128)}, f32[2048,128]{1,0:T(8,128)}, f32[256,128]{1,0:T(8,128)}) custom-call(bf16[2048,2048]{1,0:T(8,128)(2,1)} %bitcast.9, bf16[2048,896]{1,0:T(8,128)(2,1)} %bitcast.10, bf16[2048,128]{1,0:T(8,128)(2,1)} %bitcast.11, f32[1,128]{1,0:T(1,128)} %pad_bitcast_fusion.bias), custom_call_target="tpu_custom_call" | custom-call | tf_op jit(solution)/shard_map/pallas_call | solution.py:316
  165.7 0.8 slice.3
  166.6 1.5 collective-permute-start
  168.0 0.8 dynamic_slice.3
  168.8 3.8 %collective-permute-done = f32[128,128]{1,0:T(8,128)S(1)} collective-permute-done((f32[128,128]{1,0:T(8,128)S(1)}, f32[128,128]{1,0:T(8,128)S(1)}, u32[]{:S(2)}, u32[]{:S(2)}) %collective-permute-start) | collective-permute-done | bytes 65568 | tf_op jit(solution)/shard_map/ppermute | solution.py:353
  172.6 2.6 %multiply_reduce_fusion = (f32[2048]{0:T(1024)S(1)}, f32[2048,128]{1,0:T(8,128)S(1)}) fusion(f32[2048,128]{1,0:T(8,128)} %get-tuple-element.15, f32[2048,128]{1,0:T(8,128)} %get-tuple-element.16, f32[128,128]{1,0:T(8,128)S(1)} %collective-permute-done), kind=kOutput, calls=%fused_computation.2 | convolution fusion | flops 403437568 | bytes 3219456 | tf_op jit(solution)/shard_map/td,ed->te/dot_general | solution.py:357
  175.2 1.1 multiply_convert_fusion.mine
  176.3 16.0 %shard_map.66 = bf16[128,2048]{1,0:T(8,128)(2,1)} custom-call(bf16[2048,128]{1,0:T(8,128)(2,1)} %multiply_convert_fusion.mine, bf16[2048,2048]{1,0:T(8,128)(2,1)} %bitcast.8), custom_call_target="tpu_custom_call" | custom-call | tf_op jit(solution)/shard_map/pallas_call | solution.py:198
  192.4 1.9 copy.11
  (1 shorter events, 0.0 us)
Async XLA Ops:
  166.6 6.0 %collective-permute-start = (f32[128,128]{1,0:T(8,128)S(1)}, f32[128,128]{1,0:T(8,128)S(1)}, u32[]{:S(2)}, u32[]{:S(2)}) collective-permute-start(f32[128,128]{1,0:T(8,128)S(1)} %slice.3), channel_id=1, source_target_pairs={{0,16},{4,20},{8,24},{12,28},{1,17},{5,21},{9,25},{13,29},{2,18},{... | collective-permute-start | bytes 196616 | tf_op jit(solution)/shard_map/ppermute | solution.py:353
